TPU v7x, 32 devices: a whole 2x2x4 slice. The times are simulated.
32 devices in a mesh: row: 8 (over z, core), col: 4 (over y, x).
Axes of the slice: x: 2, y: 2, z: 4, core: 2. Of those that a mesh axis runs over, the one named last changes fastest.
Arguments:
- trailing: float32 [4, 8, 512, 8, 4, 512], P(None, 'row', None, None, 'col'), as said below
Outputs:
- factor: float32 [4, 8, 512, 8, 4, 512], P(None, 'row', None, None, 'col')
Inputs may be any that keep to these rules, and one draw needn't show every extreme that they name: trailing is symmetric and positive definite, with entries of at least 0.
All inputs are finite; a program needn't handle non-finite values.
Results may differ from a plain program's by a relative error of at most 0.0003.
Values sent between devices are 32-bit elements; how exact they have to be, the bound alone decides.
A program may use at most 192 MiB of HBM per device.

v0:
```python
import jax
import jax.numpy as jnp
from jax import lax
from jax.sharding import PartitionSpec as P

IB = 128
STEPS = 2


def spread(shard, axis, root):
    mine = lax.axis_index(axis) == root
    return lax.psum(jnp.where(mine, shard, jnp.zeros_like(shard)), axis)


def tri_inverse(lower_tri, block_size):
    block_count = lower_tri.shape[0] // block_size
    identity = jnp.eye(block_size, dtype=lower_tri.dtype)

    def piece_of(p, q):
        return lower_tri[
            p * block_size : (p + 1) * block_size, q * block_size : (q + 1) * block_size
        ]

    inverse = [
        [jnp.zeros((block_size, block_size), lower_tri.dtype) for q in range(block_count)]
        for p in range(block_count)
    ]
    for p in range(block_count):
        inverse[p][p] = lax.linalg.triangular_solve(
            piece_of(p, p), identity, left_side=True, lower=True
        )
    for p in range(block_count):
        for q in range(p):
            partial_sum = jnp.zeros((block_size, block_size), lower_tri.dtype)
            for s in range(q, p):
                partial_sum = partial_sum + jnp.dot(
                    piece_of(p, s), inverse[s][q], precision=lax.Precision.HIGHEST
                )
            inverse[p][q] = -jnp.dot(inverse[p][p], partial_sum, precision=lax.Precision.HIGHEST)
    return jnp.block(inverse)


def solve_panel(column, inverse):
    return jnp.einsum("iab,cb->iac", column, inverse, precision=lax.Precision.HIGHEST)


def full_update(local_tiles, panel_tiles, across, allowed):
    product = jnp.einsum("iab,jcb->iajc", panel_tiles, across, precision=lax.Precision.HIGHEST)
    return local_tiles - jnp.where(allowed[:, None, :, None], product, 0.0)


def local(trailing):
    row_tiles = trailing.shape[0]
    tile_size = trailing.shape[2]
    col_tiles = trailing.shape[3]
    n_row = lax.axis_size("row")
    n_col = lax.axis_size("col")
    row_index = lax.axis_index("row")
    col_index = lax.axis_index("col")
    local_tiles = trailing.reshape(row_tiles, tile_size, col_tiles, tile_size)
    global_rows = jnp.arange(row_tiles, dtype=jnp.int32) * n_row + row_index
    global_cols = jnp.arange(col_tiles, dtype=jnp.int32) * n_col + col_index
    column = local_tiles[:, :, 0, :]
    for k in range(STEPS):
        local_row = k // n_row
        local_col = k // n_col
        diagonal = spread(column[local_row], "row", k % n_row)
        factor_kk = jnp.linalg.cholesky(diagonal)
        solved = solve_panel(column, tri_inverse(factor_kk, IB))
        panel_tiles = spread(solved, "col", k % n_col)
        live_rows = (global_rows > k)[:, None, None]
        panel_tiles = jnp.where(live_rows, panel_tiles, 0.0)
        received = []
        for j in range(col_tiles):
            target = j * n_col + col_index
            piece_tile = lax.dynamic_index_in_dim(panel_tiles, target // n_row, 0, keepdims=False)
            received.append(spread(piece_tile, "row", target % n_row))
        across = jnp.stack(received)
        new_column = jnp.where(
            live_rows,
            panel_tiles,
            jnp.where((global_rows == k)[:, None, None], jnp.tril(factor_kk)[None], column),
        )
        local_tiles = local_tiles.at[:, :, local_col, :].set(
            jnp.where(global_cols[local_col] == k, new_column, local_tiles[:, :, local_col, :])
        )
        allowed = (global_rows[:, None] >= global_cols[None, :]) & (global_cols[None, :] > k)
        next_col = (k + 1) // n_col
        local_tiles = full_update(local_tiles, panel_tiles, across, allowed)
        if k + 1 < STEPS:
            column = local_tiles[:, :, next_col, :]
    keep_tiles = global_rows[:, None, None, None] >= global_cols[None, None, :, None]
    result = jnp.where(keep_tiles, local_tiles, 0.0)
    return result.reshape(row_tiles, 1, tile_size, col_tiles, 1, tile_size)


def solution(mesh):
    in_specs = (P(None, "row", None, None, "col", None),)
    out_specs = P(None, "row", None, None, "col", None)
    return jax.shard_map(local, mesh=mesh, in_specs=in_specs, out_specs=out_specs, check_vma=False)
```

profile of v0, /device:TPU:0, one launch (start us, length us, event | category | flops | bytes accessed | tf_op | source)
XLA Modules:
  0.0 1325.8 jit_solution(1569448012670204149)
XLA Ops:
  6.5 78.2 %copy.2 = f32[4,1,512,8,1,512]{2,5,3,0,4,1:T(8,128)} copy(f32[4,1,512,8,1,512]{5,4,3,2,1,0:T(1,128)} %param.24) | data formatting | bytes 67108864 | tf_op args[0]
  84.8 2.3 fusion.16
  87.1 78.7 %copy.34 = f32[4,1,512,8,1,512]{2,5,0,3,1,4:T(8,128)} copy(f32[4,1,512,8,1,512]{5,4,3,2,1,0:T(1,128)} %param.24) | data formatting | bytes 67108864 | tf_op jit(solution)/shard_map/reshape | solution.py:60
  165.9 1.6 copy.3
  167.4 1.4 fusion.50
  168.9 11.7 cholesky.286
  180.6 9.8 custom-call.33
  191.3 11.7 cholesky.305
  203.0 10.0 custom-call.34
  213.6 11.7 cholesky.326
  226.1 9.8 custom-call.35
  236.5 11.7 cholesky.343
  252.9 9.8 custom-call.36
  263.8 9.8 custom-call.37
  274.7 9.8 custom-call.38
  285.9 9.8 custom-call.39
  297.8 10.3 select_bitcast_fusion.1
  308.7 106.0 %all-reduce.12.cloned.1.call-done = f32[4,512,512]{1,2,0:T(8,128)} async-done(((f32[4,512,512]{1,2,0:T(8,128)}), f32[4,512,512]{1,2,0:T(8,128)}) %all-reduce.12.cloned.1.call-update) | async-done | bytes 4194320 | tf_op jit(solution)/shard_map/psum | solution.py:12
  414.7 6.7 bitcast_dynamic-update-slice_fusion
  421.4 3.7 dynamic-slice_select_fusion.8
  426.3 178.1 %all-reduce.20.cloned.1.call-done = (f32[1,512,512]{1,2,0:T(8,128)}, f32[1,512,512]{1,2,0:T(8,128)}, f32[1,512,512]{1,2,0:T(8,128)}, f32[1,512,512]{1,2,0:T(8,12...) async-done(((f32[1,512,512]{1,2,0:T(8,128)}, f32[1,512,512]{1,2,0:T(8,128)}, f32[1,512,512]{1,2,0:T(8,128)}, ...) | async-done | bytes 8388624 | tf_op jit(solution)/shard_map/psum | solution.py:12
  604.4 1.4 constant_dynamic-update-slice_fusion.7
  605.8 2.0 constant_dynamic-update-slice_fusion.6
  610.8 62.8 %select_subtract_fusion = f32[4,512,8,512]{1,3,2,0:T(8,128)} fusion(f32[4,512,8,512]{1,3,2,0:T(8,128)} %get-tuple-element.54, pred[4,8]{1,0:T(4,128)(4,1)S(1)} %broadcast_and_fusion.1, f32[8,512,512]{1,2,0:T(8,128)S(1)} %constant_dynamic-update-slice_fusion, f32[4,512,512]{1,2,0:T(8,128)S(1)} %copy-done.3), kind=kOutput, calls=%fused_computation.1 | convolution fusion | flops 51556384768 | bytes 79691808 | tf_op jit(solution)/shard_map/iab,jcb->iajc/dot_general | solution.py:48
  673.6 2.3 fusion.15
  676.4 58.7 %all-reduce.14.cloned.1.call-done = f32[512,512]{0,1:T(8,128)} async-done(((f32[512,512]{0,1:T(8,128)}), f32[512,512]{0,1:T(8,128)}) %all-reduce.14.cloned.1.call-update) | async-done | bytes 1048592 | tf_op jit(solution)/shard_map/psum | solution.py:12
  735.1 1.6 copy.13
  736.6 1.4 fusion.49
  738.1 11.7 cholesky.358
  750.0 9.8 custom-call.40
  760.5 11.7 cholesky.377
  773.6 9.9 custom-call.41
  784.2 11.7 cholesky.398
  796.6 9.8 custom-call.42
  807.0 11.7 cholesky.415
  822.5 9.8 custom-call.43
  833.4 9.8 custom-call.44
  844.3 9.8 custom-call.45
  855.5 9.8 custom-call.46
  867.3 10.6 convolution_select_fusion
  878.0 4.7 slice_bitcast_fusion
  883.0 97.9 %all-reduce.16.cloned.1.call-done = f32[4,512,512]{1,2,0:T(8,128)} async-done(((f32[4,512,512]{1,2,0:T(8,128)}), f32[4,512,512]{1,2,0:T(8,128)}) %all-reduce.16.cloned.1.call-update) | async-done | bytes 4194320 | tf_op jit(solution)/shard_map/psum | solution.py:12
  980.9 6.7 bitcast_dynamic-update-slice_fusion.1
  987.6 3.7 dynamic-slice_select_fusion
  992.2 178.3 %all-reduce.18.cloned.1.call-done = (f32[1,512,512]{1,2,0:T(8,128)}, f32[1,512,512]{1,2,0:T(8,128)}, f32[1,512,512]{1,2,0:T(8,128)}, f32[1,512,512]{1,2,0:T(8,12...) async-done(((f32[1,512,512]{1,2,0:T(8,128)}, f32[1,512,512]{1,2,0:T(8,128)}, f32[1,512,512]{1,2,0:T(8,128)}, ...) | async-done | bytes 8388624 | tf_op jit(solution)/shard_map/psum | solution.py:12
  1172.0 2.0 constant_dynamic-update-slice_fusion.14
  1176.9 63.7 %select_bitcast_fusion = f32[4,1,512,8,1,512]{2,5,3,0,4,1:T(8,128)} fusion(f32[4,512,8,512]{1,3,2,0:T(8,128)} %get-tuple-element.50, pred[4,8]{1,0:T(4,128)(4,1)S(1)} %get-tuple-element.48, pred[4,8]{1,0:T(4,128)(4,1)S(1)} %get-tuple-element.49, f32[8,512,512]{1,2,0:T(8,128)S(1)} %constant_dynamic-update-slice_fusion.8, f32[4,512,512]{1,2,0:T(8,128)S(1)} %copy-done.1), kind=kOutput, calls=%fused_computation | convolution fusion | flops 51564773376 | bytes 79691840 | tf_op jit(solution)/shard_map/iab,jcb->iajc/dot_general | solution.py:48
  1240.6 78.2 %copy.21 = f32[4,1,512,8,1,512]{5,4,3,2,1,0:T(1,128)} copy(f32[4,1,512,8,1,512]{2,5,3,0,4,1:T(8,128)} %select_bitcast_fusion) | data formatting | bytes 67108864 | tf_op jit(solution)/shard_map/reshape | solution.py:94
  (140 shorter events, 31.8 us)
Async XLA Ops:
  6.5 159.3 %all-reduce.10.cloned.1.call-start = ((), (), s32[]{:S(2)}) async-start(), calls=%async_computation | async-start | bytes 2097152 | tf_op jit(solution)/shard_map/psum | solution.py:12
  87.1 327.6 %all-reduce.12.cloned.1.call-start = ((), (), s32[]{:S(2)}) async-start(), calls=%async_computation.1 | async-start | bytes 8388608 | tf_op jit(solution)/shard_map/psum | solution.py:12
  308.0 296.3 %all-reduce.20.cloned.1.call-start = ((), (), s32[]{:S(2)}) async-start(), calls=%async_computation.5 | async-start | bytes 16777216 | tf_op jit(solution)/shard_map/psum | solution.py:12
  421.4 4.6 copy-start.2
  426.1 309.0 %all-reduce.14.cloned.1.call-start = ((), (), s32[]{:S(2)}) async-start(), calls=%async_computation.2 | async-start | bytes 2097152 | tf_op jit(solution)/shard_map/psum | solution.py:12
  604.4 6.0 copy-start.7
  604.4 6.1 copy-start.6
  604.4 6.2 copy-start.5
  604.4 6.3 copy-start.4
  604.4 6.4 copy-start.3
  676.0 304.9 %all-reduce.16.cloned.1.call-start = ((), (), s32[]{:S(2)}) async-start(), calls=%async_computation.3 | async-start | bytes 8388608 | tf_op jit(solution)/shard_map/psum | solution.py:12
  877.9 292.6 %all-reduce.18.cloned.1.call-start = ((), (), s32[]{:S(2)}) async-start(), calls=%async_computation.4 | async-start | bytes 16777216 | tf_op jit(solution)/shard_map/psum | solution.py:12
  987.6 4.6 copy-start
  1170.5 6.0 copy-start.11
  1170.5 6.1 copy-start.10
  1170.5 6.2 copy-start.9
  1170.5 6.3 copy-start.8
  1170.5 6.4 copy-start.1
Sparse Core Ops, SparseCore 0:
  87.2 61.5 all-reduce.9
  308.2 106.4 all-reduce.11
  426.2 178.1 all-reduce.19
  676.1 58.9 all-reduce.13
  878.0 102.7 all-reduce.15
  992.3 178.1 all-reduce.17
where the time goes:
time: 1340 us; the launch traced here: 1330 us
  waiting for transfers between devices  619 us (46%)
  other arithmetic  266 us (20%)
  local copies, waits for them, and re-layouts  258 us (19%)
  matrix products  162 us (12%)
  between operations  19.8 us (1%)
    psum x6, waiting for transfers between devices, spread(): return lax.psum(jnp.where(mine, shard, jnp.zeros_like(shard)), axis)  619 us
    another operation x29, other arithmetic, local(): factor_kk = jnp.linalg.cholesky(diagonal)  158 us
    dot_general x2, matrix products, full_update(): jnp.einsum('iab,jcb->iajc', panel_tiles, across, precision=lax.Precision....  126 us
    unnamed x39, local copies, waits for them, and re-layouts  92.5 us
    reshape x1, local copies, waits for them, and re-layouts, local(): local_tiles = trailing.reshape(row_tiles, tile_size, col_tiles, tile_size)  78.7 us
    another operation x10, other arithmetic, tri_inverse(): lax.linalg.triangular_solve(piece_of(p, p), identity, left_side=True, low...  78.5 us
    reshape x1, local copies, waits for them, and re-layouts, local(): return result.reshape(row_tiles, 1, tile_size, col_tiles, 1, tile_size)  78.2 us
  transfers between devices with their start and end apart: 6, of which 5 were waited for; matrix products, arithmetic and copies ran while one was open for 6% of the time, Pallas kernels for 0%

commit v1 on v0

--- a/solution.py
+++ b/solution.py
@@ -9,7 +9,7 @@
 
 def spread(shard, axis, root):
     mine = lax.axis_index(axis) == root
-    return lax.psum(jnp.where(mine, shard, jnp.zeros_like(shard)), axis)
+    return jnp.sum(lax.all_gather(jnp.where(mine, shard, jnp.zeros_like(shard)), axis), axis=0)
 
 
 def tri_inverse(lower_tri, block_size):

time: 1340 us -> 2360 us (1.76)
  waiting for transfers between devices: 619 us -> 1690 us
  local copies, waits for them, and re-layouts: 258 us -> 91.9 us
  other arithmetic: 266 us -> 380 us
    all_gather x0 -> x20, waiting for transfers between devices: none -> 1680 us  [spread(): lax.all_gather(jnp.where(mine, shard, jnp.zeros_like(shard)), axis)]
    psum x6 -> x0, waiting for transfers between devices: 619 us -> none  [spread(): return lax.psum(jnp.where(mine, shard, jnp.zeros_like(shard)), axis)]
    reduce_sum x0 -> x20, other arithmetic: none -> 109 us  [spread(): jnp.sum(lax.all_gather(jnp.where(mine, shard, jnp.zeros_like(shard)), axi...]
    reshape x1 -> x0, local copies, waits for them, and re-layouts: 78.7 us -> none  [local(): local_tiles = trailing.reshape(row_tiles, tile_size, col_tiles, tile_size)]
    unnamed x39 -> x31, local copies, waits for them, and re-layouts: 92.5 us -> 45 us
    reshape x1, local copies, waits for them, and re-layouts: 78.2 us -> 38.6 us  [local(): return result.reshape(row_tiles, 1, tile_size, col_tiles, 1, tile_size)]
  transfers between devices with their start and end apart: 6 -> 20, of which waited for: 5 -> 20; matrix products, arithmetic and copies ran while one was open for 6% -> 4% of each run, Pallas kernels for 0% -> 0%
where the time goes in v1:
time: 2360 us; the launch traced here: 2340 us
  waiting for transfers between devices  1690 us (72%)
  other arithmetic  380 us (16%)
  matrix products  165 us (7%)
  local copies, waits for them, and re-layouts  91.9 us (4%)
    all_gather x20, waiting for transfers between devices, spread(): lax.all_gather(jnp.where(mine, shard, jnp.zeros_like(shard)), axis)  1680 us
    another operation x29, other arithmetic, local(): factor_kk = jnp.linalg.cholesky(diagonal)  159 us
    dot_general x2, matrix products, full_update(): jnp.einsum('iab,jcb->iajc', panel_tiles, across, precision=lax.Precision....  124 us
    reduce_sum x20, other arithmetic, spread(): jnp.sum(lax.all_gather(jnp.where(mine, shard, jnp.zeros_like(shard)), axi...  109 us
    another operation x10, other arithmetic, tri_inverse(): lax.linalg.triangular_solve(piece_of(p, p), identity, left_side=True, low...  78.5 us
  transfers between devices with their start and end apart: 20, of which 20 were waited for; matrix products, arithmetic and copies ran while one was open for 4% of the time, Pallas kernels for 0%

profile of v1, /device:TPU:0, one launch (start us, length us, event | category | flops | bytes accessed | tf_op | source)
XLA Modules:
  0.0 2344.9 jit_solution(1226069349007535611)
XLA Ops:
  6.5 25.3 %copy.36 = f32[4,1,512,8,1,512]{5,2,0,3,4,1:T(8,128)} copy(f32[4,1,512,8,1,512]{5,4,3,2,1,0:T(1,128)} %param.24) | data formatting | bytes 67108864 | tf_op args[0]
  34.3 84.9 %all-gather.57.cloned.1.call-done = f32[8,512,1,512]{3,1,2,0:T(8,128)} async-done(((f32[1,512,1,512]{3,1,2,0:T(8,128)}), f32[8,512,1,512]{3,1,2,0:T(8,128)}) %all-gather.57.cloned.1.call-update) | async-done | bytes 8388624 | tf_op jit(solution)/shard_map/all_gather | solution.py:12
  124.2 11.7 cholesky.286
  136.1 9.8 custom-call.33
  146.6 11.9 cholesky.305
  158.5 9.8 custom-call.34
  169.0 11.7 cholesky.326
  180.7 9.8 custom-call.35
  191.1 12.1 cholesky.343
  208.1 9.8 custom-call.37
  218.8 9.8 custom-call.36
  229.7 9.8 custom-call.39
  239.7 9.8 custom-call.38
  253.1 16.5 select_bitcast_fusion.1
  275.2 155.9 %all-gather.59.cloned.1.call-done = f32[16,512,512]{2,1,0:T(8,128)} async-done(((f32[4,512,512]{2,1,0:T(8,128)}), f32[16,512,512]{2,1,0:T(8,128)}) %all-gather.59.cloned.1.call-update) | async-done | bytes 16777232 | tf_op jit(solution)/shard_map/all_gather | solution.py:12
  431.1 10.3 reduce_sum.185
  461.1 69.9 %all-gather.25.cloned.1.call-done = f32[8,512,512]{2,1,0:T(8,128)} async-done(((f32[1,512,512]{2,1,0:T(8,128)}), f32[8,512,512]{2,1,0:T(8,128)}) %all-gather.25.cloned.1.call-update) | async-done | bytes 8388624 | tf_op jit(solution)/shard_map/all_gather | solution.py:12
  535.4 77.6 %all-gather.27.cloned.1.call-done = f32[8,512,512]{2,1,0:T(8,128)} async-done(((f32[1,512,512]{2,1,0:T(8,128)}), f32[8,512,512]{2,1,0:T(8,128)}) %all-gather.27.cloned.1.call-update) | async-done | bytes 8388624 | tf_op jit(solution)/shard_map/all_gather | solution.py:12
  617.5 77.6 %all-gather.29.cloned.1.call-done = f32[8,512,512]{2,1,0:T(8,128)} async-done(((f32[1,512,512]{2,1,0:T(8,128)}), f32[8,512,512]{2,1,0:T(8,128)}) %all-gather.29.cloned.1.call-update) | async-done | bytes 8388624 | tf_op jit(solution)/shard_map/all_gather | solution.py:12
  699.6 77.6 %all-gather.31.cloned.1.call-done = f32[8,512,512]{2,1,0:T(8,128)} async-done(((f32[1,512,512]{2,1,0:T(8,128)}), f32[8,512,512]{2,1,0:T(8,128)}) %all-gather.31.cloned.1.call-update) | async-done | bytes 8388624 | tf_op jit(solution)/shard_map/all_gather | solution.py:12
  782.6 76.7 %all-gather.33.cloned.1.call-done = f32[8,512,512]{2,1,0:T(8,128)} async-done(((f32[1,512,512]{2,1,0:T(8,128)}), f32[8,512,512]{2,1,0:T(8,128)}) %all-gather.33.cloned.1.call-update) | async-done | bytes 8388624 | tf_op jit(solution)/shard_map/all_gather | solution.py:12
  864.9 76.7 %all-gather.35.cloned.1.call-done = f32[8,512,512]{2,1,0:T(8,128)} async-done(((f32[1,512,512]{2,1,0:T(8,128)}), f32[8,512,512]{2,1,0:T(8,128)}) %all-gather.35.cloned.1.call-update) | async-done | bytes 8388624 | tf_op jit(solution)/shard_map/all_gather | solution.py:12
  947.1 76.8 %all-gather.37.cloned.1.call-done = f32[8,512,512]{2,1,0:T(8,128)} async-done(((f32[1,512,512]{2,1,0:T(8,128)}), f32[8,512,512]{2,1,0:T(8,128)}) %all-gather.37.cloned.1.call-update) | async-done | bytes 8388624 | tf_op jit(solution)/shard_map/all_gather | solution.py:12
  1038.3 67.6 %all-gather.39.cloned.1.call-done = f32[8,512,512]{2,1,0:T(8,128)} async-done(((f32[1,512,512]{2,1,0:T(8,128)}), f32[8,512,512]{2,1,0:T(8,128)}) %all-gather.39.cloned.1.call-update) | async-done | bytes 8388624 | tf_op jit(solution)/shard_map/all_gather | solution.py:12
  1111.5 61.9 %select_subtract_fusion = f32[4,512,8,512]{3,1,0,2:T(8,128)} fusion(f32[4,512,8,512]{3,1,0,2:T(8,128)} %fusion.11, pred[4,8]{0,1:T(8,128)(4,1)S(1)} %get-tuple-element.82, f32[8,512,512]{2,1,0:T(8,128)} %bitcast_dynamic-update-slice_fusion.8, f32[4,512,512]{2,1,0:T(8,128)} %copy-done), kind=kOutput, calls=%fused_computation.2 | convolution fusion | flops 51556384768 | bytes 79691808 | tf_op jit(solution)/shard_map/iab,jcb->iajc/dot_general | solution.py:48
  1176.0 80.5 %all-gather.61.cloned.1.call-done = f32[8,512,1,512]{3,1,2,0:T(8,128)} async-done(((f32[1,512,1,512]{3,1,2,0:T(8,128)}), f32[8,512,1,512]{3,1,2,0:T(8,128)}) %all-gather.61.cloned.1.call-update) | async-done | bytes 8388624 | tf_op jit(solution)/shard_map/all_gather | solution.py:12
  1261.6 11.7 cholesky.358
  1273.4 9.8 custom-call.40
  1283.9 11.9 cholesky.377
  1295.9 9.8 custom-call.41
  1306.4 11.7 cholesky.398
  1318.1 9.8 custom-call.42
  1328.5 12.1 cholesky.415
  1356.8 9.8 custom-call.43
  1367.7 9.8 custom-call.46
  1391.2 9.9 fusion.18
  1401.1 156.0 %all-gather.63.cloned.1.call-done = f32[16,512,512]{2,1,0:T(8,128)} async-done(((f32[4,512,512]{2,1,0:T(8,128)}), f32[16,512,512]{2,1,0:T(8,128)}) %all-gather.63.cloned.1.call-update) | async-done | bytes 16777232 | tf_op jit(solution)/shard_map/all_gather | solution.py:12
  1557.2 10.3 reduce_sum.196
  1586.2 70.8 %all-gather.41.cloned.1.call-done = f32[8,512,512]{2,1,0:T(8,128)} async-done(((f32[1,512,512]{2,1,0:T(8,128)}), f32[8,512,512]{2,1,0:T(8,128)}) %all-gather.41.cloned.1.call-update) | async-done | bytes 8388624 | tf_op jit(solution)/shard_map/all_gather | solution.py:12
  1661.5 77.6 %all-gather.43.cloned.1.call-done = f32[8,512,512]{2,1,0:T(8,128)} async-done(((f32[1,512,512]{2,1,0:T(8,128)}), f32[8,512,512]{2,1,0:T(8,128)}) %all-gather.43.cloned.1.call-update) | async-done | bytes 8388624 | tf_op jit(solution)/shard_map/all_gather | solution.py:12
  1743.6 77.6 %all-gather.45.cloned.1.call-done = f32[8,512,512]{2,1,0:T(8,128)} async-done(((f32[1,512,512]{2,1,0:T(8,128)}), f32[8,512,512]{2,1,0:T(8,128)}) %all-gather.45.cloned.1.call-update) | async-done | bytes 8388624 | tf_op jit(solution)/shard_map/all_gather | solution.py:12
  1825.7 77.6 %all-gather.47.cloned.1.call-done = f32[8,512,512]{2,1,0:T(8,128)} async-done(((f32[1,512,512]{2,1,0:T(8,128)}), f32[8,512,512]{2,1,0:T(8,128)}) %all-gather.47.cloned.1.call-update) | async-done | bytes 8388624 | tf_op jit(solution)/shard_map/all_gather | solution.py:12
  1908.7 76.6 %all-gather.49.cloned.1.call-done = f32[8,512,512]{2,1,0:T(8,128)} async-done(((f32[1,512,512]{2,1,0:T(8,128)}), f32[8,512,512]{2,1,0:T(8,128)}) %all-gather.49.cloned.1.call-update) | async-done | bytes 8388624 | tf_op jit(solution)/shard_map/all_gather | solution.py:12
  1990.9 76.6 %all-gather.51.cloned.1.call-done = f32[8,512,512]{2,1,0:T(8,128)} async-done(((f32[1,512,512]{2,1,0:T(8,128)}), f32[8,512,512]{2,1,0:T(8,128)}) %all-gather.51.cloned.1.call-update) | async-done | bytes 8388624 | tf_op jit(solution)/shard_map/all_gather | solution.py:12
  2072.9 76.7 %all-gather.53.cloned.1.call-done = f32[8,512,512]{2,1,0:T(8,128)} async-done(((f32[1,512,512]{2,1,0:T(8,128)}), f32[8,512,512]{2,1,0:T(8,128)}) %all-gather.53.cloned.1.call-update) | async-done | bytes 8388624 | tf_op jit(solution)/shard_map/all_gather | solution.py:12
  2164.0 67.7 %all-gather.55.cloned.1.call-done = f32[8,512,512]{2,1,0:T(8,128)} async-done(((f32[1,512,512]{2,1,0:T(8,128)}), f32[8,512,512]{2,1,0:T(8,128)}) %all-gather.55.cloned.1.call-update) | async-done | bytes 8388624 | tf_op jit(solution)/shard_map/all_gather | solution.py:12
  2237.2 61.8 %select_bitcast_fusion = f32[4,1,512,8,1,512]{5,2,0,3,4,1:T(8,128)} fusion(f32[4,512,8,512]{3,1,0,2:T(8,128)} %fusion.5, pred[4,8]{0,1:T(8,128)(4,1)S(1)} %get-tuple-element.81, pred[4,8]{0,1:T(8,128)(4,1)S(1)} %get-tuple-element.80, f32[8,512,512]{2,1,0:T(8,128)} %bitcast_dynamic-update-slice_fusion, f32[4,512,512]{2,1,0:T(8,128)} %copy-done.1), kind=kOutput, calls=%fused_computation.1 | convolution fusion | flops 51564773376 | bytes 79691840 | tf_op jit(solution)/shard_map/iab,jcb->iajc/dot_general | solution.py:48
  2299.0 38.6 %copy.25 = f32[4,1,512,8,1,512]{5,4,3,2,1,0:T(1,128)} copy(f32[4,1,512,8,1,512]{5,2,0,3,4,1:T(8,128)} %select_bitcast_fusion) | data formatting | bytes 67108864 | tf_op jit(solution)/shard_map/reshape | solution.py:94
  (193 shorter events, 198.9 us)
Async XLA Ops:
  6.5 112.6 %all-gather.57.cloned.1.call-start = ((), (), s32[]{:S(2)}) async-start(), calls=%async_computation.16 | async-start | bytes 9437184 | tf_op jit(solution)/shard_map/all_gather | solution.py:12
  34.2 396.8 %all-gather.59.cloned.1.call-start = ((), (), s32[]{:S(2)}) async-start(), calls=%async_computation.17 | async-start | bytes 20971520 | tf_op jit(solution)/shard_map/all_gather | solution.py:12
  275.0 256.0 %all-gather.25.cloned.1.call-start = ((), (), s32[]{:S(2)}) async-start(), calls=%async_computation | async-start | bytes 9437184 | tf_op jit(solution)/shard_map/all_gather | solution.py:12
  444.2 4.5 copy-start
  448.7 164.3 %all-gather.27.cloned.1.call-start = ((), (), s32[]{:S(2)}) async-start(), calls=%async_computation.1 | async-start | bytes 9437184 | tf_op jit(solution)/shard_map/all_gather | solution.py:12
  449.3 245.8 %all-gather.29.cloned.1.call-start = ((), (), s32[]{:S(2)}) async-start(), calls=%async_computation.2 | async-start | bytes 9437184 | tf_op jit(solution)/shard_map/all_gather | solution.py:12
  449.9 327.3 %all-gather.31.cloned.1.call-start = ((), (), s32[]{:S(2)}) async-start(), calls=%async_computation.3 | async-start | bytes 9437184 | tf_op jit(solution)/shard_map/all_gather | solution.py:12
  450.5 408.9 %all-gather.33.cloned.1.call-start = ((), (), s32[]{:S(2)}) async-start(), calls=%async_computation.4 | async-start | bytes 9437184 | tf_op jit(solution)/shard_map/all_gather | solution.py:12
  451.2 490.4 %all-gather.35.cloned.1.call-start = ((), (), s32[]{:S(2)}) async-start(), calls=%async_computation.5 | async-start | bytes 9437184 | tf_op jit(solution)/shard_map/all_gather | solution.py:12
  452.0 571.9 %all-gather.37.cloned.1.call-start = ((), (), s32[]{:S(2)}) async-start(), calls=%async_computation.6 | async-start | bytes 9437184 | tf_op jit(solution)/shard_map/all_gather | solution.py:12
  452.7 653.2 %all-gather.39.cloned.1.call-start = ((), (), s32[]{:S(2)}) async-start(), calls=%async_computation.7 | async-start | bytes 9437184 | tf_op jit(solution)/shard_map/all_gather | solution.py:12
  453.3 803.2 %all-gather.61.cloned.1.call-start = ((), (), s32[]{:S(2)}) async-start(), calls=%async_computation.18 | async-start | bytes 9437184 | tf_op jit(solution)/shard_map/all_gather | solution.py:12
  1029.3 5.8 copy-start.2
  1029.3 6.9 copy-start.4
  1029.3 8.0 copy-start.6
  1175.7 381.4 %all-gather.63.cloned.1.call-start = ((), (), s32[]{:S(2)}) async-start(), calls=%async_computation.19 | async-start | bytes 20971520 | tf_op jit(solution)/shard_map/all_gather | solution.py:12
  1401.1 256.0 %all-gather.41.cloned.1.call-start = ((), (), s32[]{:S(2)}) async-start(), calls=%async_computation.8 | async-start | bytes 9437184 | tf_op jit(solution)/shard_map/all_gather | solution.py:12
  1570.3 4.5 copy-start.1
  1574.8 164.3 %all-gather.43.cloned.1.call-start = ((), (), s32[]{:S(2)}) async-start(), calls=%async_computation.9 | async-start | bytes 9437184 | tf_op jit(solution)/shard_map/all_gather | solution.py:12
  1575.4 245.8 %all-gather.45.cloned.1.call-start = ((), (), s32[]{:S(2)}) async-start(), calls=%async_computation.10 | async-start | bytes 9437184 | tf_op jit(solution)/shard_map/all_gather | solution.py:12
  1576.0 327.3 %all-gather.47.cloned.1.call-start = ((), (), s32[]{:S(2)}) async-start(), calls=%async_computation.11 | async-start | bytes 9437184 | tf_op jit(solution)/shard_map/all_gather | solution.py:12
  1576.6 408.8 %all-gather.49.cloned.1.call-start = ((), (), s32[]{:S(2)}) async-start(), calls=%async_computation.12 | async-start | bytes 9437184 | tf_op jit(solution)/shard_map/all_gather | solution.py:12
  1577.2 490.2 %all-gather.51.cloned.1.call-start = ((), (), s32[]{:S(2)}) async-start(), calls=%async_computation.13 | async-start | bytes 9437184 | tf_op jit(solution)/shard_map/all_gather | solution.py:12
  1577.7 571.9 %all-gather.53.cloned.1.call-start = ((), (), s32[]{:S(2)}) async-start(), calls=%async_computation.14 | async-start | bytes 9437184 | tf_op jit(solution)/shard_map/all_gather | solution.py:12
  1578.5 653.2 %all-gather.55.cloned.1.call-start = ((), (), s32[]{:S(2)}) async-start(), calls=%async_computation.15 | async-start | bytes 9437184 | tf_op jit(solution)/shard_map/all_gather | solution.py:12
  2155.1 5.7 copy-start.3
  2155.1 6.8 copy-start.5
  2155.1 7.8 copy-start.7
Sparse Core Ops, SparseCore 0:
  34.3 84.7 all-gather.56
  275.1 155.9 all-gather.58
  448.8 82.0 all-gather.24
  532.4 80.5 all-gather.26
  614.5 80.5 all-gather.28
  696.5 80.5 all-gather.30
  778.8 80.5 all-gather.32
  861.0 80.5 all-gather.34
  943.2 80.5 all-gather.36
  1025.3 80.5 all-gather.38
  1175.8 80.5 all-gather.60
  1401.2 155.9 all-gather.62
  1575.0 82.0 all-gather.40
  1658.5 80.5 all-gather.42
  1740.6 80.5 all-gather.44
  1822.6 80.5 all-gather.46
  1904.7 80.5 all-gather.48
  1986.8 80.5 all-gather.50
  2069.0 80.5 all-gather.52
  2151.1 80.5 all-gather.54
